TPU v7x, 256 devices: a whole 4x4x8 slice. The times are simulated.
256 devices in a mesh: out: 16 (over y, x), inp: 16 (over z, core).
Axes of the slice: x: 4, y: 4, z: 8, core: 2. Of those that a mesh axis runs over, the one named last changes fastest.
Arguments:
- grads: bfloat16 [2048, 28672], P('out', 'inp'), may hold values from -1.1953125 to 1.1953125
- acts: bfloat16 [2048, 8192], P('inp', 'out'), may hold values from -6 to 6
- basis_out: bfloat16 [28672, 14336], P('inp', 'out'), may hold values from -0.03125 to 0.03125
- basis_in: bfloat16 [8192, 8192], P('out', 'inp'), may hold values from -0.0625 to 0.0625
- old_correction: float32 [14336, 8192], P('out', 'inp'), may hold values from 0.1 to 2
- lengths: int32 [16], replicated, may hold values from 1 to 256, 2048 in all
Outputs:
- correction: float32 [14336, 8192], P('out', 'inp')
Inputs may be any that keep to these rules, and one draw needn't show every extreme that they name: The lengths sum to 2048; the longest example has exactly 256 tokens.
All inputs are finite; a program needn't handle non-finite values.
Results may differ from a plain program's by a relative error of at most 0.0021.
Values may be sent and summed in bfloat16 or wider, within the bound.
No kernel may reach another device: no remote copies, remote signals or barrier semaphores. Data moves between devices by JAX's collectives and lax.ppermute only.
A program may use at most 128 MiB of HBM per device.

v0:
```python
import jax
import jax.numpy as jnp
from jax import lax
from jax.sharding import PartitionSpec as P

CAP = 256


def body(grads, acts, basis_out, basis_in, old_correction, lengths):
    gathered = lax.all_gather(grads, "out", axis=0, tiled=True)
    row_count = gathered.shape[0]
    scattered = lax.psum_scatter(
        lax.dot_general(
            basis_out, gathered, (((0,), (1,)), ((), ())), preferred_element_type=jnp.float32
        ),
        "inp",
        scatter_dimension=0,
        tiled=True,
    )
    grad_rot = lax.all_gather(scattered.astype(jnp.bfloat16), "inp", axis=0, tiled=True)
    token_dim = 1
    gathered_acts = lax.all_gather(acts, "inp", axis=0, tiled=True)
    act_scattered = lax.psum_scatter(
        jnp.dot(gathered_acts, basis_in, preferred_element_type=jnp.float32),
        "out",
        scatter_dimension=0,
        tiled=True,
    )
    act_rot = lax.all_gather(act_scattered.astype(jnp.bfloat16), "out", axis=0, tiled=True)
    offsets = jnp.cumsum(lengths) - lengths
    examples = lengths.shape[0]

    def add_example(example, running):
        offset = offsets[example]
        length = lengths[example]
        first_row = jnp.minimum(offset, row_count - CAP)
        places = first_row + jnp.arange(CAP, dtype=jnp.int32)
        inside = (places >= offset) & (places < offset + length)
        grad_block = lax.dynamic_slice_in_dim(grad_rot, first_row, CAP, token_dim)
        act_block = lax.dynamic_slice_in_dim(act_rot, first_row, CAP, 0)
        act_block = jnp.where(inside[:, None], act_block, jnp.zeros((), act_block.dtype))
        projected = lax.dot_general(
            grad_block,
            act_block,
            (((token_dim,), (0,)), ((), ())),
            preferred_element_type=jnp.float32,
        )
        return running + projected * projected

    running = lax.fori_loop(0, examples, add_example, jnp.zeros(old_correction.shape, jnp.float32))
    return 0.8 * old_correction + 0.2 * running / examples


def solution(mesh):
    in_specs = (
        P("out", "inp"),
        P("inp", "out"),
        P("inp", "out"),
        P("out", "inp"),
        P("out", "inp"),
        P(),
    )
    out_specs = P("out", "inp")
    return jax.shard_map(body, mesh=mesh, in_specs=in_specs, out_specs=out_specs, check_vma=False)
```

profile of v0, /device:TPU:1, one launch (start us, length us, event | category | flops | bytes accessed | tf_op | source)
XLA Modules:
  0.0 505.1 jit_solution(16237639878966446037)
XLA Ops:
  6.5 0.7 all-gather.9.cloned.1.call-update
  7.3 0.7 all-gather.5.cloned.1.call-update
  8.1 45.1 %all-gather.9.cloned.1.call-done = bf16[2048,512]{1,0:T(8,128)(2,1)} async-done(((bf16[128,512]{1,0:T(8,128)(2,1)}), bf16[2048,512]{1,0:T(8,128)(2,1)}) %all-gather.9.cloned.1.call-update) | async-done | bytes 2097168 | tf_op jit(solution)/shard_map/all_gather | solution.py:22
  53.2 4.9 fusion.8
  58.1 66.5 %all-gather.5.cloned.1.call-done = bf16[2048,1792]{1,0:T(8,128)(2,1)} async-done(((bf16[128,1792]{1,0:T(8,128)(2,1)}), bf16[2048,1792]{1,0:T(8,128)(2,1)}) %all-gather.5.cloned.1.call-update) | async-done | bytes 7340048 | tf_op jit(solution)/shard_map/all_gather | solution.py:10
  124.7 10.9 %fusion.7 = f32[896,2048]{1,0:T(8,128)} fusion(bf16[1792,896]{1,0:T(8,128)(2,1)S(1)} %copy-done, bf16[2048,1792]{1,0:T(8,128)(2,1)} %all-gather.5.cloned.1.call-done), kind=kOutput, calls=%fused_computation.10 | convolution fusion | flops 6576668672 | bytes 17891328 | tf_op jit(solution)/shard_map/dot_general | solution.py:13
  135.7 73.4 %reduce-scatter.5.cloned.1.call-done = f32[128,512]{1,0:T(8,128)} async-done(((f32[2048,512]{1,0:T(8,128)}), f32[128,512]{1,0:T(8,128)}) %reduce-scatter.5.cloned.1.call-update) | async-done | bytes 262160 | tf_op jit(solution)/shard_map/reduce_scatter | solution.py:23
  209.1 1.6 convert_element_type.7
  210.8 67.7 %reduce-scatter.3.cloned.1.call-done = f32[56,2048]{1,0:T(8,128)} async-done(((f32[896,2048]{1,0:T(8,128)}), f32[56,2048]{1,0:T(8,128)}) %reduce-scatter.3.cloned.1.call-update) | async-done | bytes 458768 | tf_op jit(solution)/shard_map/reduce_scatter | solution.py:12
  278.4 1.7 convert_element_type.6
  280.5 51.2 %all-gather.11.cloned.1.call-done = bf16[2048,512]{1,0:T(8,128)(2,1)} async-done(((bf16[128,512]{1,0:T(8,128)(2,1)}), bf16[2048,512]{1,0:T(8,128)(2,1)}) %all-gather.11.cloned.1.call-update) | async-done | bytes 2097168 | tf_op jit(solution)/shard_map/all_gather | solution.py:29
  331.6 44.1 %all-gather.7.cloned.1.call-done = bf16[896,2048]{1,0:T(8,128)(2,1)} async-done(((bf16[56,2048]{1,0:T(8,128)(2,1)}), bf16[896,2048]{1,0:T(8,128)(2,1)}) %all-gather.7.cloned.1.call-update) | async-done | bytes 3670032 | tf_op jit(solution)/shard_map/all_gather | solution.py:20
  375.7 118.8 %while.14 = (s32[]{:T(128)}, f32[896,512]{1,0:T(8,128)}, s32[16]{0:T(128)S(1)}, bf16[896,2048]{1,0:T(8,128)(2,1)}, s32[16]{0:T(128)S(1)}, /*index=5*/bf16[2048,5...) while((s32[]{:T(128)}, f32[896,512]{1,0:T(8,128)}, s32[16]{0:T(128)S(1)}, ...), condition=%wide.region_4.5_spmd.clone, body=%wide.region_3.4_spmd.clone.sunk | while | flops 236389376 | bytes 4393164 | solution.py:50
  379.0 0.7 compare_and_fusion.2
  379.7 2.9 select_add_fusion.2
  385.8 0.7 compare_and_fusion.2
  386.5 3.5 select_add_fusion.2
  393.3 0.7 compare_and_fusion.2
  394.0 3.5 select_add_fusion.2
  400.8 0.7 compare_and_fusion.2
  401.5 3.5 select_add_fusion.2
  405.0 0.7 dynamic_slice.44
  408.2 0.7 compare_and_fusion.2
  408.9 3.5 select_add_fusion.2
  415.7 0.7 compare_and_fusion.2
  416.4 3.5 select_add_fusion.2
  423.2 0.7 compare_and_fusion.2
  423.9 3.5 select_add_fusion.2
  430.7 0.7 compare_and_fusion.2
  431.4 3.5 select_add_fusion.2
  438.2 0.7 compare_and_fusion.2
  438.9 3.5 select_add_fusion.2
  445.6 0.7 compare_and_fusion.2
  446.3 3.5 select_add_fusion.2
  453.1 0.7 compare_and_fusion.2
  453.8 3.5 select_add_fusion.2
  460.6 0.7 compare_and_fusion.2
  461.3 3.5 select_add_fusion.2
  468.1 0.7 compare_and_fusion.2
  468.8 3.5 select_add_fusion.2
  475.5 0.7 compare_and_fusion.2
  476.3 3.5 select_add_fusion.2
  479.7 0.7 dynamic_slice.44
  483.0 0.7 compare_and_fusion.2
  483.7 3.5 select_add_fusion.2
  490.4 0.7 compare_and_fusion.2
  491.1 3.5 select_add_fusion.2
  494.6 3.7 multiply_add_fusion
  (49 shorter events, 19.3 us)
Async XLA Ops:
  6.5 118.1 %copy-start = (bf16[1792,896]{1,0:T(8,128)(2,1)S(1)}, bf16[1792,896]{1,0:T(8,128)(2,1)}, u32[]{:S(2)}) copy-start(bf16[1792,896]{1,0:T(8,128)(2,1)} %param.10) | copy-start | bytes 9633796
  6.5 46.6 %all-gather.9.cloned.1.call-start = ((), (), s32[]{:S(2)}) async-start(), calls=%async_computation.5 | async-start | bytes 2228224 | tf_op jit(solution)/shard_map/all_gather | solution.py:22
  7.3 117.4 %all-gather.5.cloned.1.call-start = ((), (), s32[]{:S(2)}) async-start(), calls=%async_computation.2 | async-start | bytes 7798784 | tf_op jit(solution)/shard_map/all_gather | solution.py:10
  8.0 201.1 %reduce-scatter.5.cloned.1.call-start = ((), (), s32[]{:S(2)}) async-start(), calls=%async_computation.6 | async-start | bytes 4456448 | tf_op jit(solution)/shard_map/reduce_scatter | solution.py:23
  58.1 220.3 %reduce-scatter.3.cloned.1.call-start = ((), (), s32[]{:S(2)}) async-start(), calls=%async_computation.3 | async-start | bytes 7798784 | tf_op jit(solution)/shard_map/reduce_scatter | solution.py:12
  135.6 144.6 %copy-start.1 = (s32[16]{0:T(128)S(1)}, s32[16]{0:T(128)}, u32[]{:S(2)}) copy-start(s32[16]{0:T(128)} %param.13) | copy-start | bytes 196
  135.6 196.0 %all-gather.11.cloned.1.call-start = ((), (), s32[]{:S(2)}) async-start(), calls=%async_computation.7 | async-start | bytes 2228224 | tf_op jit(solution)/shard_map/all_gather | solution.py:29
  210.7 165.0 %all-gather.7.cloned.1.call-start = ((), (), s32[]{:S(2)}) async-start(), calls=%async_computation.4 | async-start | bytes 3899392 | tf_op jit(solution)/shard_map/all_gather | solution.py:20
Sparse Core Ops, SparseCore 0:
  9.2 43.9 all-gather.8
  55.6 69.0 all-gather.4
  128.3 80.7 reduce-scatter.4
  211.7 66.7 reduce-scatter.2
  281.0 50.5 all-gather.10
  333.5 42.2 all-gather.6
where the time goes:
time: 506 us; the launch traced here: 505 us
  waiting for transfers between devices  349 us (69%)
  matrix products  71.7 us (14%)
  loops' own time  31.7 us (6%)
  local copies, waits for them, and re-layouts  20.2 us (4%)
  other arithmetic  18.3 us (4%)
  between operations  13.5 us (3%)
    reduce_scatter x1, waiting for transfers between devices, body(): lax.psum_scatter(jnp.dot(gathered_acts, basis_in, preferred_element_type=...  73.4 us
    reduce_scatter x1, waiting for transfers between devices, body(): lax.psum_scatter(lax.dot_general(basis_out, gathered, (((0,), (1,)), ((),...  67.7 us
    all_gather x1, waiting for transfers between devices, body(): gathered = lax.all_gather(grads, 'out', axis=0, tiled=True)  66.5 us
    dot_general x16, matrix products, add_example(): lax.dot_general(grad_block, act_block, (((token_dim,), (0,)), ((), ())),...  55.9 us
    all_gather x1, waiting for transfers between devices, body(): lax.all_gather(act_scattered.astype(jnp.bfloat16), 'out', axis=0, tiled=T...  51.2 us
    all_gather x1, waiting for transfers between devices, body(): gathered_acts = lax.all_gather(acts, 'inp', axis=0, tiled=True)  45.1 us
    all_gather x1, waiting for transfers between devices, body(): lax.all_gather(scattered.astype(jnp.bfloat16), 'inp', axis=0, tiled=True)  44.1 us
    another operation x1, loops' own time, body(): lax.fori_loop(0, examples, add_example, jnp.zeros(old_correction.shape, j...  31.7 us
  transfers between devices with their start and end apart: 6, of which 6 were waited for; matrix products, arithmetic and copies ran while one was open for 4% of the time, Pallas kernels for 0%

commit v1 on v0

--- a/solution.py
+++ b/solution.py
@@ -7,7 +7,8 @@
 
 
 def body(grads, acts, basis_out, basis_in, old_correction, lengths):
-    gathered = lax.all_gather(grads, "out", axis=0, tiled=True)
+    value_now = jnp.stack([grads] * lax.axis_size("out"), axis=0)
+    gathered = jnp.concatenate(lax.all_to_all(value_now, "out", 0, 0), axis=0)
     row_count = gathered.shape[0]
     scattered = lax.psum_scatter(
         lax.dot_general(

time: 506 us -> 480 us (0.949)
  waiting for transfers between devices: 349 us -> 312 us
  starting transfers between devices: 0.2 us -> 7.8 us
    all_to_all x0 -> x1, waiting for transfers between devices: none -> 74.7 us  [body(): gathered = jnp.concatenate(lax.all_to_all(value_now, 'out', 0, 0), axis=0)]
    all_gather x1 -> x0, waiting for transfers between devices: 66.5 us -> none  [body(): gathered = lax.all_gather(grads, 'out', axis=0, tiled=True)]
    reduce_scatter x1, waiting for transfers between devices: 73.4 us -> 40.2 us  [body(): lax.psum_scatter(jnp.dot(gathered_acts, basis_in, preferred_element_type=...]
    all_gather x1, waiting for transfers between devices: 45.1 us -> 33.1 us  [body(): gathered_acts = lax.all_gather(acts, 'inp', axis=0, tiled=True)]
    all_to_all x0 -> x1, starting transfers between devices: none -> 7.63 us  [body(): gathered = jnp.concatenate(lax.all_to_all(value_now, 'out', 0, 0), axis=0)]
  transfers between devices with their start and end apart: 6 -> 6, of which waited for: 6 -> 6; matrix products, arithmetic and copies ran while one was open for 4% -> 5% of each run, Pallas kernels for 0% -> 0%
where the time goes in v1:
time: 480 us; the launch traced here: 478 us
  waiting for transfers between devices  312 us (65%)
  matrix products  71.9 us (15%)
  loops' own time  31.2 us (6%)
  local copies, waits for them, and re-layouts  25.2 us (5%)
  other arithmetic  17.1 us (4%)
  between operations  13.2 us (3%)
  starting transfers between devices  7.8 us (2%)
    all_to_all x1, waiting for transfers between devices, body(): gathered = jnp.concatenate(lax.all_to_all(value_now, 'out', 0, 0), axis=0)  74.7 us
    reduce_scatter x1, waiting for transfers between devices, body(): lax.psum_scatter(lax.dot_general(basis_out, gathered, (((0,), (1,)), ((),...  67.7 us
    dot_general x16, matrix products, add_example(): lax.dot_general(grad_block, act_block, (((token_dim,), (0,)), ((), ())),...  55.9 us
    all_gather x1, waiting for transfers between devices, body(): lax.all_gather(act_scattered.astype(jnp.bfloat16), 'out', axis=0, tiled=T...  51.4 us
    all_gather x1, waiting for transfers between devices, body(): lax.all_gather(scattered.astype(jnp.bfloat16), 'inp', axis=0, tiled=True)  44.1 us
    reduce_scatter x1, waiting for transfers between devices, body(): lax.psum_scatter(jnp.dot(gathered_acts, basis_in, preferred_element_type=...  40.2 us
    all_gather x1, waiting for transfers between devices, body(): gathered_acts = lax.all_gather(acts, 'inp', axis=0, tiled=True)  33.1 us
    another operation x1, loops' own time, body(): lax.fori_loop(0, examples, add_example, jnp.zeros(old_correction.shape, j...  31.2 us
  transfers between devices with their start and end apart: 6, of which 6 were waited for; matrix products, arithmetic and copies ran while one was open for 5% of the time, Pallas kernels for 0%

profile of v1, /device:TPU:1, one launch (start us, length us, event | category | flops | bytes accessed | tf_op | source)
XLA Modules:
  0.0 478.3 jit_solution(12800500948629236278)
XLA Ops:
  6.5 0.7 all-gather.6.cloned.1.call-update
  7.3 4.9 %stack.2 = bf16[16,128,1792]{2,1,0:T(8,128)(2,1)} broadcast(bf16[128,1792]{1,0:T(8,128)(2,1)} %param.8), dimensions={1,2} | broadcast | bytes 7798784 | tf_op jit(solution)/shard_map/stack | solution.py:10
  12.2 7.6 %all-to-all-start = ((bf16[16,128,1792]{2,1,0:T(8,128)(2,1)}), bf16[16,128,1792]{2,1,0:T(8,128)(2,1)}, u32[]{:S(2)}, u32[]{:S(2)}) async-start(bf16[16,128,1792]{2,1,0:T(8,128)(2,1)} %stack.2), calls=%async_computation | async-start | bytes 14680064 | tf_op jit(solution)/shard_map/all_to_all | solution.py:11
  19.9 33.1 %all-gather.6.cloned.1.call-done = bf16[2048,512]{1,0:T(8,128)(2,1)} async-done(((bf16[128,512]{1,0:T(8,128)(2,1)}), bf16[2048,512]{1,0:T(8,128)(2,1)}) %all-gather.6.cloned.1.call-update) | async-done | bytes 2097168 | tf_op jit(solution)/shard_map/all_gather | solution.py:23
  53.0 4.9 %fusion.8 = f32[2048,512]{1,0:T(8,128)} fusion(bf16[2048,512]{1,0:T(8,128)(2,1)} %all-gather.6.cloned.1.call-done, bf16[512,512]{1,0:T(8,128)(2,1)} %param.11), kind=kOutput, calls=%fused_computation.11 | convolution fusion | flops 1073741824 | bytes 6815744 | tf_op jit(solution)/shard_map/dot_general | solution.py:25
  58.0 74.7 %all-to-all-done = bf16[16,128,1792]{2,1,0:T(8,128)(2,1)} async-done(((bf16[16,128,1792]{2,1,0:T(8,128)(2,1)}), bf16[16,128,1792]{2,1,0:T(8,128)(2,1)}, u32[]{:S(2)}, u32[]{:S(2)}) %all-to-all-start) | async-done | bytes 7340064 | tf_op jit(solution)/shard_map/all_to_all | solution.py:11
  132.7 11.1 %fusion.7 = f32[896,2048]{1,0:T(8,128)} fusion(bf16[1792,896]{1,0:T(8,128)(2,1)S(1)} %copy-done, bf16[2048,1792]{1,0:T(8,128)(2,1)} %bitcast.1), kind=kOutput, calls=%fused_computation.10 | convolution fusion | flops 6576668672 | bytes 17891328 | tf_op jit(solution)/shard_map/dot_general | solution.py:14
  143.9 40.2 %reduce-scatter.5.cloned.1.call-done = f32[128,512]{1,0:T(8,128)} async-done(((f32[2048,512]{1,0:T(8,128)}), f32[128,512]{1,0:T(8,128)}) %reduce-scatter.5.cloned.1.call-update) | async-done | bytes 262160 | tf_op jit(solution)/shard_map/reduce_scatter | solution.py:24
  184.1 1.6 convert_element_type.7
  185.8 67.7 %reduce-scatter.3.cloned.1.call-done = f32[56,2048]{1,0:T(8,128)} async-done(((f32[896,2048]{1,0:T(8,128)}), f32[56,2048]{1,0:T(8,128)}) %reduce-scatter.3.cloned.1.call-update) | async-done | bytes 458768 | tf_op jit(solution)/shard_map/reduce_scatter | solution.py:13
  253.5 1.7 convert_element_type.6
  255.5 51.4 %all-gather.8.cloned.1.call-done = bf16[2048,512]{1,0:T(8,128)(2,1)} async-done(((bf16[128,512]{1,0:T(8,128)(2,1)}), bf16[2048,512]{1,0:T(8,128)(2,1)}) %all-gather.8.cloned.1.call-update) | async-done | bytes 2097168 | tf_op jit(solution)/shard_map/all_gather | solution.py:30
  306.8 44.1 %all-gather.4.cloned.1.call-done = bf16[896,2048]{1,0:T(8,128)(2,1)} async-done(((bf16[56,2048]{1,0:T(8,128)(2,1)}), bf16[896,2048]{1,0:T(8,128)(2,1)}) %all-gather.4.cloned.1.call-update) | async-done | bytes 3670032 | tf_op jit(solution)/shard_map/all_gather | solution.py:21
  350.9 117.1 %while.14 = (s32[]{:T(128)}, f32[896,512]{1,0:T(8,128)}, s32[16]{0:T(128)S(1)}, bf16[896,2048]{1,0:T(8,128)(2,1)}, s32[16]{0:T(128)S(1)}, /*index=5*/bf16[2048,5...) while((s32[]{:T(128)}, f32[896,512]{1,0:T(8,128)}, s32[16]{0:T(128)S(1)}, ...), condition=%wide.region_4.5_spmd.clone, body=%wide.region_3.4_spmd.clone.sunk | while | flops 236389376 | bytes 4393164 | solution.py:51
  352.2 0.7 dynamic_slice.45
  354.1 0.6 compare_and_fusion.2
  354.8 2.9 select_add_fusion.2
  358.9 0.7 dynamic_slice.45
  361.5 3.5 select_add_fusion.2
  366.3 0.7 dynamic_slice.45
  368.9 3.5 select_add_fusion.2
  373.6 0.7 dynamic_slice.45
  376.2 3.5 select_add_fusion.2
  381.0 0.7 dynamic_slice.45
  383.6 3.5 select_add_fusion.2
  388.4 0.7 dynamic_slice.45
  391.0 3.5 select_add_fusion.2
  395.7 0.7 dynamic_slice.45
  398.4 3.5 select_add_fusion.2
  403.1 0.7 dynamic_slice.45
  405.7 3.5 select_add_fusion.2
  410.5 0.7 dynamic_slice.45
  413.1 3.5 select_add_fusion.2
  417.9 0.7 dynamic_slice.45
  420.5 3.5 select_add_fusion.2
  425.2 0.7 dynamic_slice.45
  427.8 3.5 select_add_fusion.2
  432.6 0.7 dynamic_slice.45
  435.2 3.5 select_add_fusion.2
  440.0 0.7 dynamic_slice.45
  442.6 3.5 select_add_fusion.2
  447.3 0.7 dynamic_slice.45
  449.9 3.5 select_add_fusion.2
  454.6 0.7 dynamic_slice.45
  457.2 3.5 select_add_fusion.2
  461.9 0.7 dynamic_slice.45
  464.5 3.5 select_add_fusion.2
  468.0 3.7 multiply_add_fusion
  (49 shorter events, 19.2 us)
Async XLA Ops:
  6.5 126.2 %copy-start = (bf16[1792,896]{1,0:T(8,128)(2,1)S(1)}, bf16[1792,896]{1,0:T(8,128)(2,1)}, u32[]{:S(2)}) copy-start(bf16[1792,896]{1,0:T(8,128)(2,1)} %param.10) | copy-start | bytes 9633796
  6.5 46.5 %all-gather.6.cloned.1.call-start = ((), (), s32[]{:S(2)}) async-start(), calls=%async_computation.5 | async-start | bytes 2228224 | tf_op jit(solution)/shard_map/all_gather | solution.py:23
  12.2 120.5 %all-to-all-start = ((bf16[16,128,1792]{2,1,0:T(8,128)(2,1)}), bf16[16,128,1792]{2,1,0:T(8,128)(2,1)}, u32[]{:S(2)}, u32[]{:S(2)}) async-start(bf16[16,128,1792]{2,1,0:T(8,128)(2,1)} %stack.2), calls=%async_computation | async-start | bytes 14680064 | tf_op jit(solution)/shard_map/all_to_all | solution.py:11
  19.8 164.3 %reduce-scatter.5.cloned.1.call-start = ((), (), s32[]{:S(2)}) async-start(), calls=%async_computation.6 | async-start | bytes 4456448 | tf_op jit(solution)/shard_map/reduce_scatter | solution.py:24
  57.9 195.5 %reduce-scatter.3.cloned.1.call-start = ((), (), s32[]{:S(2)}) async-start(), calls=%async_computation.3 | async-start | bytes 7798784 | tf_op jit(solution)/shard_map/reduce_scatter | solution.py:13
  143.8 111.4 %copy-start.1 = (s32[16]{0:T(128)S(1)}, s32[16]{0:T(128)}, u32[]{:S(2)}) copy-start(s32[16]{0:T(128)} %param.13) | copy-start | bytes 196
  143.8 163.0 %all-gather.8.cloned.1.call-start = ((), (), s32[]{:S(2)}) async-start(), calls=%async_computation.7 | async-start | bytes 2228224 | tf_op jit(solution)/shard_map/all_gather | solution.py:30
  185.7 165.2 %all-gather.4.cloned.1.call-start = ((), (), s32[]{:S(2)}) async-start(), calls=%async_computation.4 | async-start | bytes 3899392 | tf_op jit(solution)/shard_map/all_gather | solution.py:21
Sparse Core Ops, SparseCore 0:
  9.2 43.7 all-gather.5
  58.1 125.9 reduce-scatter.4
  186.8 66.5 reduce-scatter.2
  256.1 50.7 all-gather.7
  308.7 42.2 all-gather.3
